TPU v7x, 128 devices: a whole 4x4x4 slice. The times are simulated.
128 devices in a mesh: arc: 8 (over y, x_hi), trow: 4 (over z), tcol: 4 (over x_lo, core).
Axes of the slice: x: 4 (x_hi: 2, x_lo: 2; x = x_hi * 2 + x_lo), y: 4, z: 4, core: 2. Of those that a mesh axis runs over, the one named last changes fastest.
Arguments:
- design: bfloat16 [5120, 8192], P('arc', 'tcol'), may hold values from -0.125 to 0.125
- local_design: bfloat16 [5120, 128], P('arc'), may hold values from -0.3125 to 0.3125
- lengths: int32 [16], P('arc'), may hold values from 1 to 320, 3840 in all
- regularizer: float32 [8192], P(('arc', 'trow')), may hold values from 0.2 to 2
Outputs:
- normal: float32 [8192, 8192], P(('arc', 'trow'), 'tcol')
- panel_factor: float32 [2, 8192, 512], P(None, 'tcol')
Inputs may be any that keep to these rules, and one draw needn't show every extreme that they name: `lengths`: each arc has at least one live row; some arc is full.
All inputs are finite; a program needn't handle non-finite values. No bound on the sum of `lengths` on one device may be relied on, other than what follows from the above.
Results may differ from a plain program's by a relative error of at most 0.003.
Values may be sent and summed in bfloat16 or wider, within the bound.
A program may use at most 128 MiB of HBM per device.

v0:
```python
import jax
import jax.numpy as jnp
from jax import lax
from jax.sharding import PartitionSpec as P

PANEL = 512
PANELS = 2
ridge = 0.1


def broadcast(block, axis, holder):
    block = jnp.where(lax.axis_index(axis) == holder, block, jnp.zeros_like(block))
    return lax.psum(block, axis)


def project_arcs(design, local_design, lengths):
    arc_count = lengths.shape[0]
    row_count = design.shape[0]
    capacity = row_count // arc_count
    arc_blocks = design.reshape(arc_count, capacity, design.shape[1])
    local_half = local_design.reshape(arc_count, capacity, local_design.shape[1])
    live_rows = jnp.arange(capacity, dtype=jnp.int32)[None, :] < lengths[:, None]
    arc_blocks = jnp.where(live_rows[:, :, None], arc_blocks, jnp.zeros((), design.dtype))
    local_half = jnp.where(live_rows[:, :, None], local_half, jnp.zeros((), local_design.dtype))
    local_normal = jnp.einsum(
        "acl,acm->alm", local_half, local_half, preferred_element_type=jnp.float32
    )
    local_normal = local_normal + ridge * jnp.eye(local_half.shape[2], dtype=jnp.float32)[None]
    local_factor = jnp.linalg.cholesky(local_normal)
    local_cols = local_half.astype(jnp.float32)
    basis_rows = lax.linalg.triangular_solve(
        local_factor, jnp.transpose(local_cols, (0, 2, 1)), left_side=True, lower=True
    )
    basis_rows = basis_rows.astype(jnp.bfloat16)
    loadings = jnp.einsum(
        "alc,acw->alw", basis_rows, arc_blocks, preferred_element_type=jnp.float32
    ).astype(jnp.bfloat16)
    cleaned = arc_blocks.astype(jnp.float32) - jnp.einsum(
        "alc,alw->acw", basis_rows, loadings, preferred_element_type=jnp.float32
    )
    return cleaned.astype(jnp.bfloat16).reshape(row_count, design.shape[1])


def contract_rows(left_rows, right_rows):
    return lax.dot_general(
        left_rows, right_rows, (((0,), (0,)), ((), ())), preferred_element_type=jnp.float32
    )


def per_device(design, local_design, lengths, regularizer):
    row_count, col_width = design.shape
    tile_rows = regularizer.shape[0]
    arc_total = lax.axis_size("arc")
    trow_total = lax.axis_size("trow")
    trow_index = lax.axis_index("trow")
    row_start = (lax.axis_index("arc") * trow_total + trow_index) * tile_rows
    col_start = lax.axis_index("tcol") * col_width
    projected = project_arcs(design, local_design, lengths)
    gathered = lax.all_gather(projected, "tcol", axis=1, tiled=True)
    regrouped = gathered.reshape(row_count, arc_total, trow_total, tile_rows)
    selected = lax.dynamic_slice_in_dim(regrouped, trow_index, 1, 2).reshape(
        row_count, arc_total * tile_rows
    )
    normal_block = lax.psum_scatter(
        contract_rows(selected, projected), "arc", scatter_dimension=0, tiled=True
    )
    rows_global = row_start + jnp.arange(tile_rows, dtype=jnp.int32)
    cols_global = col_start + jnp.arange(col_width, dtype=jnp.int32)
    on_diagonal = rows_global[:, None] == cols_global[None, :]
    normal_block = normal_block + jnp.where(
        on_diagonal, regularizer[:, None], jnp.zeros((), jnp.float32)
    )
    panel_factors = []
    for panel_index in range(PANELS):
        lead_col = panel_index * PANEL
        padded_rows = jnp.pad(normal_block, ((PANEL, PANEL), (0, 0)))
        slice_start = jnp.clip(lead_col - row_start + PANEL, 0, tile_rows + PANEL)
        slice_rows = lax.dynamic_slice_in_dim(padded_rows, slice_start, PANEL, 0)
        panel_global = lead_col + jnp.arange(PANEL, dtype=jnp.int32)
        in_tile = (panel_global >= row_start) & (panel_global < row_start + tile_rows)
        own_share = jnp.where(in_tile[:, None], slice_rows, jnp.zeros((), jnp.float32))
        panel_strip = lax.psum(own_share, ("arc", "trow"))
        pivot_block, row_strip = (
            broadcast(panel_strip[:, lead_col : lead_col + PANEL], "tcol", 0),
            broadcast(normal_block[:, lead_col : lead_col + PANEL], "tcol", 0),
        )
        lower_factor = jnp.linalg.cholesky(pivot_block)
        col_factor = lax.linalg.triangular_solve(
            lower_factor, panel_strip, left_side=True, lower=True
        ).T
        row_factor = lax.linalg.triangular_solve(
            lower_factor, row_strip.T, left_side=True, lower=True
        ).T
        col_factor = jnp.where(
            cols_global[:, None] >= lead_col, col_factor, jnp.zeros((), jnp.float32)
        )
        row_factor = jnp.where(
            rows_global[:, None] >= lead_col, row_factor, jnp.zeros((), jnp.float32)
        )
        normal_block = normal_block - jnp.dot(
            row_factor, col_factor.T, precision=lax.Precision.HIGHEST
        )
        panel_factors.append(col_factor)
    return (normal_block, jnp.stack(panel_factors))


def solution(mesh):
    return jax.shard_map(
        per_device,
        mesh=mesh,
        in_specs=(P("arc", "tcol"), P("arc", None), P("arc"), P(("arc", "trow"))),
        out_specs=(P(("arc", "trow"), "tcol"), P(None, "tcol", None)),
        check_vma=False,
    )
```

profile of v0, /device:TPU:1, one launch (start us, length us, event | category | flops | bytes accessed | tf_op | source)
XLA Modules:
  0.0 1569.1 jit_solution(3386765637183662593)
XLA Ops:
  9.6 23.5 %custom-call.33 = f32[2,128,128]{2,1,0:T(8,128)S(1)} custom-call(f32[2,128,128]{2,1,0:T(8,128)S(1)} %fusion.97), custom_call_target="Cholesky" | custom-call | tf_op jit(solution)/shard_map/jit(cholesky)/cholesky | solution.py:29
  33.4 19.7 %custom-call.34 = f32[2,1,128,128]{2,3,1,0:T(8,128)S(1)} custom-call(f32[2,1,128,128]{3,2,1,0:T(8,128)S(1)} %select_bitcast_fusion), custom_call_target="InvertDiagBlocksLowerTriangular" | custom-call | tf_op jit(solution)/shard_map/triangular_solve | solution.py:31
  54.3 4.0 subtract_convert_fusion
  58.4 2.6 copy.63
  61.2 102.4 %all-gather.2.cloned.1.call-done = bf16[640,8192]{0,1:T(8,128)(2,1)} async-done(((bf16[640,2048]{0,1:T(8,128)(2,1)}), bf16[640,8192]{0,1:T(8,128)(2,1)}) %all-gather.2.cloned.1.call-update) | async-done | bytes 10485776 | tf_op jit(solution)/shard_map/all_gather | solution.py:59
  163.6 2.0 constant_dynamic-slice_fusion.2
  165.6 10.2 fusion.158
  175.9 190.4 %reduce-scatter.2.cloned.1.call-done = f32[256,2048]{0,1:T(8,128)} async-done(((f32[2048,2048]{0,1:T(8,128)}), f32[256,2048]{0,1:T(8,128)}) %reduce-scatter.2.cloned.1.call-update) | async-done | bytes 2097168 | tf_op jit(solution)/shard_map/reduce_scatter | solution.py:64
  368.0 3.2 fusion
  372.1 345.6 %all-reduce.10.cloned.1.call-done = f32[512,2048]{0,1:T(8,128)} async-done(((f32[512,2048]{0,1:T(8,128)}), f32[512,2048]{0,1:T(8,128)}) %all-reduce.10.cloned.1.call-update) | async-done | bytes 4194320 | tf_op jit(solution)/shard_map/psum | solution.py:82
  717.8 2.3 slice_select_fusion.1
  720.2 71.5 %all-reduce.16.cloned.1.call-done = (f32[512,512]{0,1:T(8,128)}, f32[512,256]{1,0:T(8,128)}) async-done(((f32[512,512]{0,1:T(8,128)}, f32[512,256]{1,0:T(8,128)}), (f32[512,512]{0,1:T(8,128)}, f32[512,256]{1,0:T(8,128)})) %all-reduce.16.cloned.1.call-update) | async-done | bytes 1572880 | tf_op jit(solution)/shard_map/psum | solution.py:13
  794.7 11.7 cholesky.327
  806.6 9.8 custom-call.40
  817.1 11.7 cholesky.346
  828.8 10.2 custom-call.41
  839.7 11.7 cholesky.367
  851.5 9.8 custom-call.42
  861.9 11.7 cholesky.384
  878.9 7.7 while.8
  886.6 39.3 %custom-call.43 = f32[4,128,128]{1,2,0:T(8,128)S(1)} custom-call(f32[4,128,128]{2,1,0:T(8,128)S(1)} %get-tuple-element.33), custom_call_target="InvertDiagBlocksLowerTriangular" | custom-call | tf_op jit(solution)/shard_map/triangular_solve/custom-call.9 | solution.py:91
  926.0 2.3 fusion.36
  929.6 3.0 convolution_subtract_fusion.5
  935.1 4.7 convolution_subtract_fusion.3
  942.2 7.2 fusion.17
  955.5 3.9 convolution_subtract_fusion.1
  960.7 3.2 fusion.1
  963.9 2.1 fusion.40
  966.0 342.8 %all-reduce.12.cloned.1.call-done = f32[512,2048]{0,1:T(8,128)} async-done(((f32[512,2048]{0,1:T(8,128)}), f32[512,2048]{0,1:T(8,128)}) %all-reduce.12.cloned.1.call-update) | async-done | bytes 4194320 | tf_op jit(solution)/shard_map/psum | solution.py:82
  1308.8 2.3 slice_select_fusion
  1311.2 3.4 fusion.21
  1314.6 68.2 %all-reduce.14.cloned.1.call-done = (f32[512,512]{0,1:T(8,128)}, f32[512,256]{1,0:T(8,128)}) async-done(((f32[512,512]{0,1:T(8,128)}, f32[512,256]{1,0:T(8,128)}), (f32[512,512]{0,1:T(8,128)}, f32[512,256]{1,0:T(8,128)})) %all-reduce.14.cloned.1.call-update) | async-done | bytes 1572880 | tf_op jit(solution)/shard_map/psum | solution.py:13
  1385.7 11.7 cholesky.399
  1397.6 9.8 custom-call.45
  1408.1 11.7 cholesky.418
  1419.8 10.2 custom-call.46
  1430.7 11.7 cholesky.439
  1442.5 9.8 custom-call.47
  1452.9 11.7 cholesky.456
  1469.9 7.7 while.9
  1477.6 39.3 %custom-call.48 = f32[4,128,128]{1,2,0:T(8,128)S(1)} custom-call(f32[4,128,128]{2,1,0:T(8,128)S(1)} %get-tuple-element.35), custom_call_target="InvertDiagBlocksLowerTriangular" | custom-call | tf_op jit(solution)/shard_map/triangular_solve/custom-call.9 | solution.py:91
  1517.0 2.3 fusion.34
  1520.6 3.0 convolution_subtract_fusion.4
  1526.0 4.7 convolution_subtract_fusion.2
  1533.2 7.1 fusion.14
  1546.2 2.2 fusion.20
  1548.7 3.7 convolution_subtract_fusion
  1554.2 7.8 pad_maximum_fusion
  (168 shorter events, 65.9 us)
Async XLA Ops:
  7.2 156.4 %all-gather.2.cloned.1.call-start = ((), (), s32[]{:S(2)}) async-start(), calls=%async_computation.1 | async-start | bytes 13107200 | tf_op jit(solution)/shard_map/all_gather | solution.py:59
  61.0 305.3 %reduce-scatter.2.cloned.1.call-start = ((), (), s32[]{:S(2)}) async-start(), calls=%async_computation.2 | async-start | bytes 18874368 | tf_op jit(solution)/shard_map/reduce_scatter | solution.py:64
  175.8 190.5 %copy-start.18 = (f32[256]{0:T(256)S(1)}, f32[256]{0:T(256)}, u32[]{:S(2)}) copy-start(f32[256]{0:T(256)} %param.12) | copy-start | bytes 3076
  175.8 542.0 %all-reduce.10.cloned.1.call-start = ((), (), s32[]{:S(2)}) async-start(), calls=%async_computation.3 | async-start | bytes 8388608 | tf_op jit(solution)/shard_map/psum | solution.py:82
  368.0 3.3 copy-start
  371.2 420.5 %all-reduce.16.cloned.1.call-start = ((), (), s32[]{:S(2)}) async-start(), calls=%async_computation.6 | async-start | bytes 3145728 | tf_op jit(solution)/shard_map/psum | solution.py:13
  720.1 588.7 %all-reduce.12.cloned.1.call-start = ((), (), s32[]{:S(2)}) async-start(), calls=%async_computation.4 | async-start | bytes 8388608 | tf_op jit(solution)/shard_map/psum | solution.py:82
  886.6 48.4 %copy-start.3 = (f32[512,512]{1,0:T(8,128)}, f32[512,512]{1,0:T(8,128)S(1)}, u32[]{:S(2)}) copy-start(f32[512,512]{1,0:T(8,128)S(1)} %get-tuple-element.206) | copy-start | bytes 3145732
  942.2 8.3 copy-start.16
  942.2 13.2 copy-start.1
  942.2 13.2 copy-start.4
  942.2 13.2 copy-start.6
  942.2 13.2 copy-start.8
  950.5 8.9 copy-start.10
  959.4 1.3 copy-start.14
  963.9 347.3 %copy-start.5 = (f32[128,2048]{0,1:T(8,128)S(1)}, f32[128,2048]{0,1:T(8,128)}, u32[]{:S(2)}) copy-start(f32[128,2048]{0,1:T(8,128)} %copy.69) | copy-start | bytes 3145732
  963.9 347.3 %copy-start.7 = (f32[128,2048]{0,1:T(8,128)S(1)}, f32[128,2048]{0,1:T(8,128)}, u32[]{:S(2)}) copy-start(f32[128,2048]{0,1:T(8,128)} %copy.70) | copy-start | bytes 3145732
  963.9 347.3 %copy-start.9 = (f32[128,2048]{0,1:T(8,128)S(1)}, f32[128,2048]{0,1:T(8,128)}, u32[]{:S(2)}) copy-start(f32[128,2048]{0,1:T(8,128)} %copy.71) | copy-start | bytes 3145732
  963.9 418.8 %all-reduce.14.cloned.1.call-start = ((), (), s32[]{:S(2)}) async-start(), calls=%async_computation.5 | async-start | bytes 3145728 | tf_op jit(solution)/shard_map/psum | solution.py:13
  1477.6 48.4 %copy-start.2 = (f32[512,512]{1,0:T(8,128)}, f32[512,512]{1,0:T(8,128)S(1)}, u32[]{:S(2)}) copy-start(f32[512,512]{1,0:T(8,128)S(1)} %get-tuple-element.205) | copy-start | bytes 3145732
  1533.2 8.1 copy-start.17
  1533.2 13.0 copy-start.11
  1533.2 13.0 copy-start.12
  1533.2 13.0 copy-start.13
  1546.2 2.5 copy-start.15
Sparse Core Ops, SparseCore 0:
  61.1 102.4 all-gather.1
  175.9 190.3 reduce-scatter.1
  371.4 346.3 all-reduce.9
  721.0 70.6 all-reduce.15
  964.0 344.7 all-reduce.11
  1312.0 70.6 all-reduce.13
where the time goes:
time: 1580 us; the launch traced here: 1570 us
  waiting for transfers between devices  1120 us (71%)
  other arithmetic  314 us (20%)
  matrix products  78.7 us (5%)
  local copies, waits for them, and re-layouts  34.9 us (2%)
  between operations  20 us (1%)
    psum x2, waiting for transfers between devices, per_device(): panel_strip = lax.psum(own_share, ('arc', 'trow'))  688 us
    reduce_scatter x1, waiting for transfers between devices, per_device(): lax.psum_scatter(contract_rows(selected, projected), 'arc', scatter_dimen...  190 us
    another operation x30, other arithmetic, per_device(): lower_factor = jnp.linalg.cholesky(pivot_block)  159 us
    psum x2, waiting for transfers between devices, broadcast(): return lax.psum(block, axis)  140 us
    all_gather x1, waiting for transfers between devices, per_device(): gathered = lax.all_gather(projected, 'tcol', axis=1, tiled=True)  102 us
    another operation x5, other arithmetic, per_device(): lax.linalg.triangular_solve(lower_factor, row_strip.T, left_side=True, lo...  79.2 us
    another operation x14, matrix products, per_device(): lax.linalg.triangular_solve(lower_factor, panel_strip, left_side=True, lo...  40.7 us
  transfers between devices with their start and end apart: 6, of which 6 were waited for; matrix products, arithmetic and copies ran while one was open for 0% of the time, Pallas kernels for 0%

commit v1 on v0

--- a/solution.py
+++ b/solution.py
@@ -79,7 +79,8 @@
         panel_global = lead_col + jnp.arange(PANEL, dtype=jnp.int32)
         in_tile = (panel_global >= row_start) & (panel_global < row_start + tile_rows)
         own_share = jnp.where(in_tile[:, None], slice_rows, jnp.zeros((), jnp.float32))
-        panel_strip = lax.psum(own_share, ("arc", "trow"))
+        half = lax.psum(own_share, "arc")
+        panel_strip = lax.psum(half, "trow")
         pivot_block, row_strip = (
             broadcast(panel_strip[:, lead_col : lead_col + PANEL], "tcol", 0),
             broadcast(normal_block[:, lead_col : lead_col + PANEL], "tcol", 0),

time: 1580 us -> 1410 us (0.89)
  waiting for transfers between devices: 1120 us -> 948 us
    psum x2 -> x4, waiting for transfers between devices: 688 us -> 559 us  [the longest x2 372 us: per_device(): half = lax.psum(own_share, 'arc')]
    psum x2, waiting for transfers between devices: 140 us -> 96.2 us  [broadcast(): return lax.psum(block, axis)]
  transfers between devices with their start and end apart: 6 -> 8, of which waited for: 6 -> 8; matrix products, arithmetic and copies ran while one was open for 0% -> 0% of each run, Pallas kernels for 0% -> 0%
where the time goes in v1:
time: 1410 us; the launch traced here: 1400 us
  waiting for transfers between devices  948 us (67%)
  other arithmetic  314 us (22%)
  matrix products  78.7 us (6%)
  local copies, waits for them, and re-layouts  35.5 us (3%)
  between operations  20.3 us (1%)
    psum x2, waiting for transfers between devices, per_device(): half = lax.psum(own_share, 'arc')  372 us
    reduce_scatter x1, waiting for transfers between devices, per_device(): lax.psum_scatter(contract_rows(selected, projected), 'arc', scatter_dimen...  190 us
    psum x2, waiting for transfers between devices, per_device(): panel_strip = lax.psum(half, 'trow')  186 us
    another operation x30, other arithmetic, per_device(): lower_factor = jnp.linalg.cholesky(pivot_block)  159 us
    all_gather x1, waiting for transfers between devices, per_device(): gathered = lax.all_gather(projected, 'tcol', axis=1, tiled=True)  102 us
    psum x2, waiting for transfers between devices, broadcast(): return lax.psum(block, axis)  96.2 us
    another operation x5, other arithmetic, per_device(): lax.linalg.triangular_solve(lower_factor, row_strip.T, left_side=True, lo...  79.2 us
    another operation x14, matrix products, per_device(): lax.linalg.triangular_solve(lower_factor, panel_strip, left_side=True, lo...  40.7 us
  transfers between devices with their start and end apart: 8, of which 8 were waited for; matrix products, arithmetic and copies ran while one was open for 0% of the time, Pallas kernels for 0%

profile of v1, /device:TPU:1, one launch (start us, length us, event | category | flops | bytes accessed | tf_op | source)
XLA Modules:
  0.0 1397.5 jit_solution(984631654632649256)
XLA Ops:
  9.6 23.5 %custom-call.33 = f32[2,128,128]{2,1,0:T(8,128)S(1)} custom-call(f32[2,128,128]{2,1,0:T(8,128)S(1)} %fusion.97), custom_call_target="Cholesky" | custom-call | tf_op jit(solution)/shard_map/jit(cholesky)/cholesky | solution.py:29
  33.4 19.7 %custom-call.34 = f32[2,1,128,128]{2,3,1,0:T(8,128)S(1)} custom-call(f32[2,1,128,128]{3,2,1,0:T(8,128)S(1)} %select_bitcast_fusion), custom_call_target="InvertDiagBlocksLowerTriangular" | custom-call | tf_op jit(solution)/shard_map/triangular_solve | solution.py:31
  54.3 4.0 subtract_convert_fusion
  58.4 2.6 copy.63
  61.2 102.4 %all-gather.2.cloned.1.call-done = bf16[640,8192]{0,1:T(8,128)(2,1)} async-done(((bf16[640,2048]{0,1:T(8,128)(2,1)}), bf16[640,8192]{0,1:T(8,128)(2,1)}) %all-gather.2.cloned.1.call-update) | async-done | bytes 10485776 | tf_op jit(solution)/shard_map/all_gather | solution.py:59
  165.6 10.2 fusion.158
  175.9 190.4 %reduce-scatter.2.cloned.1.call-done = f32[256,2048]{0,1:T(8,128)} async-done(((f32[2048,2048]{0,1:T(8,128)}), f32[256,2048]{0,1:T(8,128)}) %reduce-scatter.2.cloned.1.call-update) | async-done | bytes 2097168 | tf_op jit(solution)/shard_map/reduce_scatter | solution.py:64
  368.0 3.2 fusion
  371.3 187.1 %all-reduce.12.cloned.1.call-done = f32[512,2048]{0,1:T(8,128)} async-done(((f32[512,2048]{0,1:T(8,128)}), f32[512,2048]{0,1:T(8,128)}) %all-reduce.12.cloned.1.call-update) | async-done | bytes 4194320 | tf_op jit(solution)/shard_map/psum | solution.py:82
  559.4 93.8 %all-reduce.14.cloned.1.call-done = f32[512,2048]{0,1:T(8,128)} async-done(((f32[512,2048]{0,1:T(8,128)}), f32[512,2048]{0,1:T(8,128)}) %all-reduce.14.cloned.1.call-update) | async-done | bytes 4194320 | tf_op jit(solution)/shard_map/psum | solution.py:83
  653.2 2.3 slice_select_fusion.1
  655.8 49.5 %all-reduce.22.cloned.1.call-done = (f32[512,512]{0,1:T(8,128)}, f32[512,256]{1,0:T(8,128)}) async-done(((f32[512,512]{0,1:T(8,128)}, f32[512,256]{1,0:T(8,128)}), (f32[512,512]{0,1:T(8,128)}, f32[512,256]{1,0:T(8,128)})) %all-reduce.22.cloned.1.call-update) | async-done | bytes 1572880 | tf_op jit(solution)/shard_map/psum | solution.py:13
  708.4 11.7 cholesky.327
  720.2 9.8 custom-call.40
  730.7 11.7 cholesky.346
  742.5 10.2 custom-call.41
  753.4 11.7 cholesky.367
  765.1 9.8 custom-call.42
  775.6 11.7 cholesky.384
  792.9 7.9 while.8
  800.8 39.3 %custom-call.43 = f32[4,128,128]{1,2,0:T(8,128)S(1)} custom-call(f32[4,128,128]{2,1,0:T(8,128)S(1)} %get-tuple-element.33), custom_call_target="InvertDiagBlocksLowerTriangular" | custom-call | tf_op jit(solution)/shard_map/triangular_solve/custom-call.9 | solution.py:92
  840.1 2.3 fusion.36
  843.7 3.0 convolution_subtract_fusion.5
  849.1 4.7 convolution_subtract_fusion.3
  856.4 7.2 fusion.17
  869.6 3.9 convolution_subtract_fusion.1
  874.9 3.2 fusion.1
  878.1 185.3 %all-reduce.16.cloned.1.call-done = f32[512,2048]{0,1:T(8,128)} async-done(((f32[512,2048]{0,1:T(8,128)}), f32[512,2048]{0,1:T(8,128)}) %all-reduce.16.cloned.1.call-update) | async-done | bytes 4194320 | tf_op jit(solution)/shard_map/psum | solution.py:82
  1065.5 92.7 %all-reduce.18.cloned.1.call-done = f32[512,2048]{0,1:T(8,128)} async-done(((f32[512,2048]{0,1:T(8,128)}), f32[512,2048]{0,1:T(8,128)}) %all-reduce.18.cloned.1.call-update) | async-done | bytes 4194320 | tf_op jit(solution)/shard_map/psum | solution.py:83
  1158.2 2.3 slice_select_fusion
  1160.6 3.4 fusion.21
  1164.0 46.7 %all-reduce.20.cloned.1.call-done = (f32[512,512]{0,1:T(8,128)}, f32[512,256]{1,0:T(8,128)}) async-done(((f32[512,512]{0,1:T(8,128)}, f32[512,256]{1,0:T(8,128)}), (f32[512,512]{0,1:T(8,128)}, f32[512,256]{1,0:T(8,128)})) %all-reduce.20.cloned.1.call-update) | async-done | bytes 1572880 | tf_op jit(solution)/shard_map/psum | solution.py:13
  1213.7 11.7 cholesky.399
  1225.5 9.8 custom-call.45
  1236.0 11.7 cholesky.418
  1247.8 10.2 custom-call.46
  1258.7 11.7 cholesky.439
  1270.4 9.8 custom-call.47
  1280.8 11.7 cholesky.456
  1298.0 8.0 while.9
  1306.1 39.3 %custom-call.48 = f32[4,128,128]{1,2,0:T(8,128)S(1)} custom-call(f32[4,128,128]{2,1,0:T(8,128)S(1)} %get-tuple-element.35), custom_call_target="InvertDiagBlocksLowerTriangular" | custom-call | tf_op jit(solution)/shard_map/triangular_solve/custom-call.9 | solution.py:92
  1345.4 2.3 fusion.34
  1349.0 3.0 convolution_subtract_fusion.4
  1354.4 4.7 convolution_subtract_fusion.2
  1361.7 7.1 fusion.14
  1374.7 2.2 fusion.20
  1377.1 3.7 convolution_subtract_fusion
  1382.6 7.8 pad_maximum_fusion
  (174 shorter events, 71.1 us)
Async XLA Ops:
  7.2 156.4 %all-gather.2.cloned.1.call-start = ((), (), s32[]{:S(2)}) async-start(), calls=%async_computation.1 | async-start | bytes 13107200 | tf_op jit(solution)/shard_map/all_gather | solution.py:59
  61.0 305.3 %reduce-scatter.2.cloned.1.call-start = ((), (), s32[]{:S(2)}) async-start(), calls=%async_computation.2 | async-start | bytes 18874368 | tf_op jit(solution)/shard_map/reduce_scatter | solution.py:64
  175.8 190.5 %copy-start.18 = (f32[256]{0:T(256)S(1)}, f32[256]{0:T(256)}, u32[]{:S(2)}) copy-start(f32[256]{0:T(256)} %param.12) | copy-start | bytes 3076
  175.8 382.7 %all-reduce.12.cloned.1.call-start = ((), (), s32[]{:S(2)}) async-start(), calls=%async_computation.3 | async-start | bytes 8388608 | tf_op jit(solution)/shard_map/psum | solution.py:82
  368.0 190.5 %copy-start = (f32[256,2048]{0,1:T(8,128)}, f32[256,2048]{0,1:T(8,128)S(1)}, u32[]{:S(2)}) copy-start(f32[256,2048]{0,1:T(8,128)S(1)} %select_add_fusion) | copy-start | bytes 6291460
  371.2 282.0 %all-reduce.14.cloned.1.call-start = ((), (), s32[]{:S(2)}) async-start(), calls=%async_computation.4 | async-start | bytes 8388608 | tf_op jit(solution)/shard_map/psum | solution.py:83
  558.5 146.9 %all-reduce.22.cloned.1.call-start = ((), (), s32[]{:S(2)}) async-start(), calls=%async_computation.8 | async-start | bytes 3145728 | tf_op jit(solution)/shard_map/psum | solution.py:13
  655.5 407.9 %all-reduce.16.cloned.1.call-start = ((), (), s32[]{:S(2)}) async-start(), calls=%async_computation.5 | async-start | bytes 8388608 | tf_op jit(solution)/shard_map/psum | solution.py:82
  800.8 48.4 %copy-start.3 = (f32[512,512]{1,0:T(8,128)}, f32[512,512]{1,0:T(8,128)S(1)}, u32[]{:S(2)}) copy-start(f32[512,512]{1,0:T(8,128)S(1)} %get-tuple-element.208) | copy-start | bytes 3145732
  856.4 8.3 copy-start.16
  856.4 13.2 copy-start.1
  856.4 13.2 copy-start.4
  856.4 13.2 copy-start.6
  856.4 13.2 copy-start.8
  864.6 8.9 copy-start.10
  873.5 1.3 copy-start.14
  878.1 280.1 %all-reduce.18.cloned.1.call-start = ((), (), s32[]{:S(2)}) async-start(), calls=%async_computation.6 | async-start | bytes 8388608 | tf_op jit(solution)/shard_map/psum | solution.py:83
  1063.4 97.1 %copy-start.5 = (f32[128,2048]{0,1:T(8,128)S(1)}, f32[128,2048]{0,1:T(8,128)}, u32[]{:S(2)}) copy-start(f32[128,2048]{0,1:T(8,128)} %copy.69) | copy-start | bytes 3145732
  1063.4 97.1 %copy-start.7 = (f32[128,2048]{0,1:T(8,128)S(1)}, f32[128,2048]{0,1:T(8,128)}, u32[]{:S(2)}) copy-start(f32[128,2048]{0,1:T(8,128)} %copy.70) | copy-start | bytes 3145732
  1063.4 97.1 %copy-start.9 = (f32[128,2048]{0,1:T(8,128)S(1)}, f32[128,2048]{0,1:T(8,128)}, u32[]{:S(2)}) copy-start(f32[128,2048]{0,1:T(8,128)} %copy.71) | copy-start | bytes 3145732
  1063.4 147.2 %all-reduce.20.cloned.1.call-start = ((), (), s32[]{:S(2)}) async-start(), calls=%async_computation.7 | async-start | bytes 3145728 | tf_op jit(solution)/shard_map/psum | solution.py:13
  1306.0 48.4 %copy-start.2 = (f32[512,512]{1,0:T(8,128)}, f32[512,512]{1,0:T(8,128)S(1)}, u32[]{:S(2)}) copy-start(f32[512,512]{1,0:T(8,128)S(1)} %get-tuple-element.207) | copy-start | bytes 3145732
  1361.7 8.1 copy-start.17
  1361.7 13.0 copy-start.11
  1361.7 13.0 copy-start.12
  1361.7 13.0 copy-start.13
  1374.7 2.5 copy-start.15
Sparse Core Ops, SparseCore 0:
  61.1 102.4 all-gather.1
  175.9 190.3 reduce-scatter.1
  371.4 187.0 all-reduce.11
  560.8 92.3 all-reduce.13
  656.2 49.0 all-reduce.21
  878.2 185.1 all-reduce.15
  1065.8 92.3 all-reduce.17
  1161.5 49.0 all-reduce.19
